TPU v7x, 32 devices: a whole 2x2x4 slice. The times are simulated.
32 devices in a mesh: group: 8 (over y, x, core), replica: 4 (over z).
Axes of the slice: x: 2, y: 2, z: 4, core: 2. Of those that a mesh axis runs over, the one named last changes fastest.
Arguments:
- tokens: bfloat16 [4, 1024, 960], P('replica', 'group'), may hold values from -6 to 6
- positions: int32 [4, 1024], P('replica', 'group'), may hold values from 0 to 999, as said below
- gain_attn: bfloat16 [2, 960], P(None, 'group'), may hold values from 0.5 to 1.5
- w_query: bfloat16 [2, 960, 960], P(None, 'group'), may hold values from -0.1875 to 0.1875
- w_key: bfloat16 [2, 960, 320], P(None, 'group'), may hold values from -0.1875 to 0.1875
- w_value: bfloat16 [2, 960, 320], P(None, 'group'), may hold values from -0.1875 to 0.1875
- w_out: bfloat16 [2, 960, 960], P(None, 'group'), may hold values from -0.5 to 0.5
- gain_ffn: bfloat16 [2, 960], P(None, 'group'), may hold values from 0.5 to 1.5
- w_gate: bfloat16 [2, 960, 2560], P(None, 'group'), may hold values from -0.1875 to 0.1875
- w_up: bfloat16 [2, 960, 2560], P(None, 'group'), may hold values from -0.1875 to 0.1875
- w_down: bfloat16 [2, 2560, 960], P(None, 'group'), may hold values from -0.125 to 0.125
- cotangent: bfloat16 [4, 1024, 960], P('replica', 'group'), may hold values from -6 to 6
Outputs:
- activations: float32 [4, 2, 1024, 960], P('replica', None, 'group')
- grad_tokens: float32 [4, 1024, 960], P('replica', 'group')
- grad_gain_attn: float32 [2, 960], P(None, 'group')
- grad_w_query: float32 [2, 960, 960], P(None, 'group')
- grad_w_key: float32 [2, 960, 320], P(None, 'group')
- grad_w_value: float32 [2, 960, 320], P(None, 'group')
- grad_w_out: float32 [2, 960, 960], P(None, 'group')
- grad_gain_ffn: float32 [2, 960], P(None, 'group')
- grad_w_gate: float32 [2, 960, 2560], P(None, 'group')
- grad_w_up: float32 [2, 960, 2560], P(None, 'group')
- grad_w_down: float32 [2, 2560, 960], P(None, 'group')
Inputs may be any that keep to these rules, and one draw needn't show every extreme that they name: In each sequence positions are 0 at a document's first token and rise by one per token inside a document; every document except a sequence's last has 100 to 1000 tokens; the first token of every sequence has position 0.
All inputs are finite; a program needn't handle non-finite values.
Results may differ from a plain program's by a relative error of at most 0.02.
Values may be sent and summed in bfloat16 or wider, within the bound.
A program may use at most 320 MiB of HBM per device.

v0:
```python
import jax
import jax.numpy as jnp
from jax import lax
from jax.sharding import PartitionSpec as P

HEADS = 15
KV_HEADS = 5
HEAD_DIM = 64
LAYERS = 2
epsilon = 1e-05
rope_base = 100000.0


def forward_dot(left, right):
    return jnp.dot(left, right, preferred_element_type=jnp.float32)


def over_rows(left, right):
    return lax.dot_general(
        left, right, (((0,), (0,)), ((), ())), preferred_element_type=jnp.float32
    )


def against(left, right):
    return lax.dot_general(
        left, right, (((1,), (1,)), ((), ())), preferred_element_type=jnp.float32
    )


def rope_tables(token_positions):
    half_dim = HEAD_DIM // 2
    frequency = rope_base ** (-2.0 * jnp.arange(half_dim, dtype=jnp.float32) / HEAD_DIM)
    angles = token_positions.astype(jnp.float32)[:, None] * frequency[None, :]
    return (jnp.cos(angles)[:, None, :], jnp.sin(angles)[:, None, :])


def rotate(vectors, cosine, sine_table):
    half_dim = HEAD_DIM // 2
    leading, trailing = (vectors[..., :half_dim], vectors[..., half_dim:])
    return jnp.concatenate(
        [leading * cosine - trailing * sine_table, trailing * cosine + leading * sine_table],
        axis=-1,
    )


def rotate_back(vectors, cosine, sine_table):
    half_dim = HEAD_DIM // 2
    leading, trailing = (vectors[..., :half_dim], vectors[..., half_dim:])
    return jnp.concatenate(
        [leading * cosine + trailing * sine_table, trailing * cosine - leading * sine_table],
        axis=-1,
    )


def norm_forward(stream):
    inverse = lax.rsqrt(jnp.mean(stream * stream, axis=-1, keepdims=True) + epsilon)
    return (inverse, stream * inverse)


def norm_back(grad_unit, unit_value, inverse):
    return inverse * (
        grad_unit - unit_value * jnp.mean(grad_unit * unit_value, axis=-1, keepdims=True)
    )


def masked_scores(grouped, key_all, allowed):
    scores = (
        jnp.einsum("qkgd,skd->kgqs", grouped, key_all, preferred_element_type=jnp.float32) * 0.125
    )
    return jnp.where(allowed[None, None], scores, -1e30)


def layer_forward(stream, gathered, allowed, cosine, sine_table):
    gain_attn, w_query, w_key, w_value, w_out, gain_ffn, w_gate, w_up, w_down = gathered
    row_count = stream.shape[0]
    inverse_attn, unit_attn = norm_forward(stream)
    normed_attn = (unit_attn * gain_attn.astype(jnp.float32)).astype(jnp.bfloat16)
    queries = rotate(
        forward_dot(normed_attn, w_query).reshape(row_count, HEADS, HEAD_DIM), cosine, sine_table
    ).astype(jnp.bfloat16)
    own_keys = rotate(
        forward_dot(normed_attn, w_key).reshape(row_count, KV_HEADS, HEAD_DIM), cosine, sine_table
    ).astype(jnp.bfloat16)
    own_values = (
        forward_dot(normed_attn, w_value)
        .astype(jnp.bfloat16)
        .reshape(row_count, KV_HEADS, HEAD_DIM)
    )
    key_all, value_all = (
        lax.all_gather(own_keys, "group", axis=0, tiled=True),
        lax.all_gather(own_values, "group", axis=0, tiled=True),
    )
    grouped = queries.reshape(row_count, KV_HEADS, HEADS // KV_HEADS, HEAD_DIM)
    scores = masked_scores(grouped, key_all, allowed)
    row_max = jnp.max(scores, axis=-1, keepdims=True)
    exponent = jnp.exp(scores - row_max)
    row_total = jnp.sum(exponent, axis=-1, keepdims=True)
    weights_low = (exponent / row_total).astype(jnp.bfloat16)
    mixed_heads = jnp.einsum(
        "kgqs,skd->qkgd", weights_low, value_all, preferred_element_type=jnp.float32
    )
    mixed_heads = mixed_heads.reshape(row_count, HEADS * HEAD_DIM).astype(jnp.bfloat16)
    after_attn = stream + forward_dot(mixed_heads, w_out)
    inverse_ffn, unit_ffn = norm_forward(after_attn)
    normed_ffn = (unit_ffn * gain_ffn.astype(jnp.float32)).astype(jnp.bfloat16)
    gate_value = forward_dot(normed_ffn, w_gate)
    up_value = forward_dot(normed_ffn, w_up)
    hidden = (jax.nn.silu(gate_value) * up_value).astype(jnp.bfloat16)
    result = after_attn + forward_dot(hidden, w_down)
    saved = (
        unit_attn,
        inverse_attn,
        normed_attn,
        grouped,
        row_max,
        row_total,
        mixed_heads,
        unit_ffn,
        inverse_ffn,
        normed_ffn,
        gate_value,
        up_value,
        hidden,
    )
    return (result, saved, (own_keys, own_values), (key_all, value_all))


def replica_total(shares):
    (
        share_gain_attn,
        share_query,
        share_key,
        share_value,
        share_out,
        share_gain_ffn,
        share_gate,
        share_up,
        share_down,
    ) = shares
    return lax.psum(
        (
            share_gain_attn,
            share_query,
            share_key,
            share_value,
            share_out,
            share_gain_ffn,
            share_gate,
            share_up,
            share_down,
        ),
        "replica",
    )


def owned_columns(matrix, owner, members):
    width = matrix.shape[1] // members
    return lax.dynamic_slice_in_dim(matrix, owner * width, width, 1)


def layer_backward(grad_result, gathered, saved, key_all, value_all, allowed, cosine, sine_table):
    gain_attn, w_query, w_key, w_value, w_out, gain_ffn, w_gate, w_up, w_down = gathered
    (
        unit_attn,
        inverse_attn,
        normed_attn,
        grouped,
        row_max,
        row_total,
        mixed_heads,
        unit_ffn,
        inverse_ffn,
        normed_ffn,
        gate_value,
        up_value,
        hidden,
    ) = saved
    row_count = grad_result.shape[0]
    branch_low = grad_result.astype(jnp.bfloat16)
    grad_hidden = against(branch_low, w_down)
    sigmoid_gate = jax.nn.sigmoid(gate_value)
    grad_up_low = (grad_hidden * gate_value * sigmoid_gate).astype(jnp.bfloat16)
    grad_gate_low = (
        grad_hidden * up_value * sigmoid_gate * (1.0 + gate_value * (1.0 - sigmoid_gate))
    ).astype(jnp.bfloat16)
    grad_normed_ffn = against(grad_gate_low, w_gate) + against(grad_up_low, w_up)
    grad_gain_ffn = jnp.sum(grad_normed_ffn * unit_ffn, axis=0)
    grad_after = grad_result + norm_back(
        grad_normed_ffn * gain_ffn.astype(jnp.float32), unit_ffn, inverse_ffn
    )
    after_low = grad_after.astype(jnp.bfloat16)
    grad_mixed = (
        against(after_low, w_out)
        .astype(jnp.bfloat16)
        .reshape(row_count, KV_HEADS, HEADS // KV_HEADS, HEAD_DIM)
    )
    scores = masked_scores(grouped, key_all, allowed)
    weights_soft = jnp.exp(scores - row_max) / row_total
    grad_weights = jnp.einsum(
        "qkgd,skd->kgqs", grad_mixed, value_all, preferred_element_type=jnp.float32
    )
    grad_value_all = jnp.einsum(
        "kgqs,qkgd->skd",
        weights_soft.astype(jnp.bfloat16),
        grad_mixed,
        preferred_element_type=jnp.float32,
    )
    grad_scores = (
        weights_soft * (grad_weights - jnp.sum(grad_weights * weights_soft, axis=-1, keepdims=True))
    ).astype(jnp.bfloat16)
    grad_queries = (
        jnp.einsum("kgqs,skd->qkgd", grad_scores, key_all, preferred_element_type=jnp.float32)
        * 0.125
    )
    grad_key_all = (
        jnp.einsum("kgqs,qkgd->skd", grad_scores, grouped, preferred_element_type=jnp.float32)
        * 0.125
    )
    grad_keys, grad_values = (
        lax.psum_scatter(grad_key_all, "group", scatter_dimension=0, tiled=True),
        lax.psum_scatter(grad_value_all, "group", scatter_dimension=0, tiled=True),
    )
    query_back = rotate_back(grad_queries.reshape(row_count, HEADS, HEAD_DIM), cosine, sine_table)
    query_back = query_back.reshape(row_count, HEADS * HEAD_DIM).astype(jnp.bfloat16)
    key_back = (
        rotate_back(grad_keys, cosine, sine_table)
        .reshape(row_count, KV_HEADS * HEAD_DIM)
        .astype(jnp.bfloat16)
    )
    value_back = grad_values.reshape(row_count, KV_HEADS * HEAD_DIM).astype(jnp.bfloat16)
    grad_normed_attn = (
        against(query_back, w_query) + against(key_back, w_key) + against(value_back, w_value)
    )
    grad_gain_attn = jnp.sum(grad_normed_attn * unit_attn, axis=0)
    grad_stream = grad_after + norm_back(
        grad_normed_attn * gain_attn.astype(jnp.float32), unit_attn, inverse_attn
    )
    owner = lax.axis_index("group")
    members = lax.axis_size("group")
    piece_attn = lax.all_gather(normed_attn, "group", axis=0, tiled=True)
    piece_query = lax.all_gather(query_back, "group", axis=0, tiled=True)
    piece_key = lax.all_gather(key_back, "group", axis=0, tiled=True)
    piece_value = lax.all_gather(value_back, "group", axis=0, tiled=True)
    piece_mixed = lax.all_gather(mixed_heads, "group", axis=0, tiled=True)
    piece_after = lax.all_gather(after_low, "group", axis=0, tiled=True)
    piece_ffn = lax.all_gather(normed_ffn, "group", axis=0, tiled=True)
    piece_gate = lax.all_gather(grad_gate_low, "group", axis=0, tiled=True)
    piece_up = lax.all_gather(grad_up_low, "group", axis=0, tiled=True)
    piece_hidden = lax.all_gather(hidden, "group", axis=0, tiled=True)
    piece_branch = lax.all_gather(branch_low, "group", axis=0, tiled=True)
    left_attn = owned_columns(piece_attn, owner, members)
    left_mixed = owned_columns(piece_mixed, owner, members)
    left_ffn = owned_columns(piece_ffn, owner, members)
    left_hidden = owned_columns(piece_hidden, owner, members)
    gain_shares = (
        lax.psum_scatter(grad_gain_attn, "group", scatter_dimension=0, tiled=True),
        lax.psum_scatter(grad_gain_ffn, "group", scatter_dimension=0, tiled=True),
    )
    shares = (
        gain_shares[0],
        over_rows(left_attn, piece_query),
        over_rows(left_attn, piece_key),
        over_rows(left_attn, piece_value),
        over_rows(left_mixed, piece_after),
        gain_shares[1],
        over_rows(left_ffn, piece_gate),
        over_rows(left_ffn, piece_up),
        over_rows(left_hidden, piece_branch),
    )
    return (grad_stream, shares)


def on_device(
    tokens,
    positions,
    gain_attn,
    w_query,
    w_key,
    w_value,
    w_out,
    gain_ffn,
    w_gate,
    w_up,
    w_down,
    cotangent,
):
    row_count = tokens.shape[1]
    length_all = row_count * lax.axis_size("group")
    row_index = lax.axis_index("group") * row_count + jnp.arange(row_count, dtype=jnp.int32)
    token_positions = positions[0]
    key_index = jnp.arange(length_all, dtype=jnp.int32)
    allowed = (key_index[None, :] <= row_index[:, None]) & (
        key_index[None, :] >= (row_index - token_positions)[:, None]
    )
    cosine, sine_table = rope_tables(token_positions)
    stream = tokens[0].astype(jnp.float32)
    saved_all = []
    own_all = []
    full_all = []
    gathered_all = []
    outputs = []
    for layer_index in range(LAYERS):
        gathered = (
            lax.all_gather(gain_attn[layer_index], "group", axis=0, tiled=True),
            lax.all_gather(w_query[layer_index], "group", axis=0, tiled=True),
            lax.all_gather(w_key[layer_index], "group", axis=0, tiled=True),
            lax.all_gather(w_value[layer_index], "group", axis=0, tiled=True),
            lax.all_gather(w_out[layer_index], "group", axis=0, tiled=True),
            lax.all_gather(gain_ffn[layer_index], "group", axis=0, tiled=True),
            lax.all_gather(w_gate[layer_index], "group", axis=0, tiled=True),
            lax.all_gather(w_up[layer_index], "group", axis=0, tiled=True),
            lax.all_gather(w_down[layer_index], "group", axis=0, tiled=True),
        )
        stream, saved, own_pair, full_pair = layer_forward(
            stream, gathered, allowed, cosine, sine_table
        )
        saved_all.append(saved)
        own_all.append(own_pair)
        full_all.append(full_pair)
        gathered_all.append(gathered)
        outputs.append(stream)
    grad_stream = cotangent[0].astype(jnp.float32)
    owned = [None] * LAYERS
    for layer_index in reversed(range(LAYERS)):
        gathered = (
            lax.all_gather(gain_attn[layer_index], "group", axis=0, tiled=True),
            lax.all_gather(w_query[layer_index], "group", axis=0, tiled=True),
            lax.all_gather(w_key[layer_index], "group", axis=0, tiled=True),
            lax.all_gather(w_value[layer_index], "group", axis=0, tiled=True),
            lax.all_gather(w_out[layer_index], "group", axis=0, tiled=True),
            lax.all_gather(gain_ffn[layer_index], "group", axis=0, tiled=True),
            lax.all_gather(w_gate[layer_index], "group", axis=0, tiled=True),
            lax.all_gather(w_up[layer_index], "group", axis=0, tiled=True),
            lax.all_gather(w_down[layer_index], "group", axis=0, tiled=True),
        )
        key_all, value_all = (
            lax.all_gather(own_all[layer_index][0], "group", axis=0, tiled=True),
            lax.all_gather(own_all[layer_index][1], "group", axis=0, tiled=True),
        )
        grad_stream, shares = layer_backward(
            grad_stream,
            gathered,
            saved_all[layer_index],
            key_all,
            value_all,
            allowed,
            cosine,
            sine_table,
        )
        owned[layer_index] = replica_total(shares)
    stacked = tuple(
        (
            jnp.stack([owned[layer_index][member] for layer_index in range(LAYERS)])
            for member in range(9)
        )
    )
    activations = jnp.stack(outputs)[None]
    return (
        activations,
        grad_stream[None],
        stacked[0],
        stacked[1],
        stacked[2],
        stacked[3],
        stacked[4],
        stacked[5],
        stacked[6],
        stacked[7],
        stacked[8],
    )


def solution(mesh):
    in_specs = (
        P("replica", "group", None),
        P("replica", "group"),
        P(None, "group"),
        P(None, "group", None),
        P(None, "group", None),
        P(None, "group", None),
        P(None, "group", None),
        P(None, "group"),
        P(None, "group", None),
        P(None, "group", None),
        P(None, "group", None),
        P("replica", "group", None),
    )
    out_specs = (
        P("replica", None, "group", None),
        P("replica", "group", None),
        P(None, "group"),
        P(None, "group", None),
        P(None, "group", None),
        P(None, "group", None),
        P(None, "group", None),
        P(None, "group"),
        P(None, "group", None),
        P(None, "group", None),
        P(None, "group", None),
    )
    return jax.shard_map(
        on_device, mesh=mesh, in_specs=in_specs, out_specs=out_specs, check_vma=False
    )
```

profile of v0, /device:TPU:0, one launch (start us, length us, event | category | flops | bytes accessed | tf_op | source)
XLA Modules:
  0.0 1593.5 jit_solution(1129092299961670674)
XLA Ops:
  21.1 15.6 all-reduce.11
  64.5 13.1 all-gather.1
  80.3 13.3 all_gather.156
  95.9 20.1 %all-gather.11 = bf16[1,960,320]{2,0,1:T(2,128)(2,1)S(1)} all-gather(bf16[1,120,320]{2,0,1:T(2,128)(2,1)S(1)} %copy.82), channel_id=13, replica_groups=mesh['group'=8,'replica'=4] {'group'}, dimensions={1}, use_global_device_ids=true | all-gather | bytes 691200 | tf_op jit(solution)/shard_map/all_gather | solution.py:306
  119.7 12.5 all-gather.10
  166.6 38.7 %all-gather.90.cloned.1.call-done = bf16[1,2560,960]{2,1,0:T(8,128)(2,1)} async-done(((bf16[1,320,960]{2,1,0:T(8,128)(2,1)}), bf16[1,2560,960]{2,1,0:T(8,128)(2,1)}) %all-gather.90.cloned.1.call-update) | async-done | bytes 4915216 | tf_op jit(solution)/shard_map/all_gather | solution.py:312
  224.0 14.7 all_gather.167
  252.6 16.1 %all-gather.94.cloned.1.call-done = bf16[1,960,960]{2,1,0:T(8,128)(2,1)} async-done(((bf16[1,120,960]{2,1,0:T(8,128)(2,1)}), bf16[1,960,960]{2,1,0:T(8,128)(2,1)}) %all-gather.94.cloned.1.call-update) | async-done | bytes 1843216 | tf_op jit(solution)/shard_map/all_gather | solution.py:308
  271.7 39.3 %all-gather.98.cloned.1.call-done = bf16[1,960,2560]{2,1,0:T(8,128)(2,1)} async-done(((bf16[1,120,2560]{2,1,0:T(8,128)(2,1)}), bf16[1,960,2560]{2,1,0:T(8,128)(2,1)}) %all-gather.98.cloned.1.call-update) | async-done | bytes 4915216 | tf_op jit(solution)/shard_map/all_gather | solution.py:311
  315.3 39.3 %all-gather.100.cloned.1.call-done = bf16[1,2560,960]{2,1,0:T(8,128)(2,1)} async-done(((bf16[1,320,960]{2,1,0:T(8,128)(2,1)}), bf16[1,2560,960]{2,1,0:T(8,128)(2,1)}) %all-gather.100.cloned.1.call-update) | async-done | bytes 4915216 | tf_op jit(solution)/shard_map/all_gather | solution.py:312
  360.0 36.1 %all-gather.96.cloned.1.call-done = bf16[1,960,2560]{2,1,0:T(8,128)(2,1)} async-done(((bf16[1,120,2560]{2,1,0:T(8,128)(2,1)}), bf16[1,960,2560]{2,1,0:T(8,128)(2,1)}) %all-gather.96.cloned.1.call-update) | async-done | bytes 4915216 | tf_op jit(solution)/shard_map/all_gather | solution.py:310
  446.0 25.5 %reduce-scatter.5.cloned.1.call-done = f32[128,5,64]{0,2,1:T(8,128)} async-done(((f32[1024,5,64]{0,2,1:T(8,128)}), f32[128,5,64]{0,2,1:T(8,128)}) %reduce-scatter.5.cloned.1.call-update) | async-done | bytes 163856 | tf_op jit(solution)/shard_map/reduce_scatter | solution.py:220
  474.8 37.7 %reduce-scatter.7.cloned.1.call-done = f32[128,5,64]{0,2,1:T(8,128)} async-done(((f32[1024,5,64]{0,2,1:T(8,128)}), f32[128,5,64]{0,2,1:T(8,128)}) %reduce-scatter.7.cloned.1.call-update) | async-done | bytes 163856 | tf_op jit(solution)/shard_map/reduce_scatter | solution.py:221
  588.1 12.7 all_gather.183
  608.2 25.1 %all-gather.60.cloned.1.call-done = bf16[1024,960]{0,1:T(8,128)(2,1)} async-done(((bf16[128,960]{0,1:T(8,128)(2,1)}), bf16[1024,960]{0,1:T(8,128)(2,1)}) %all-gather.60.cloned.1.call-update) | async-done | bytes 1966096 | tf_op jit(solution)/shard_map/all_gather | solution.py:244
  636.5 37.8 %reduce-scatter.11.cloned.1.call-done = f32[128,5,64]{0,2,1:T(8,128)} async-done(((f32[1024,5,64]{0,2,1:T(8,128)}), f32[128,5,64]{0,2,1:T(8,128)}) %reduce-scatter.11.cloned.1.call-update) | async-done | bytes 163856 | tf_op jit(solution)/shard_map/reduce_scatter | solution.py:221
  675.2 40.1 %reduce-scatter.9.cloned.1.call-done = f32[128,5,64]{0,2,1:T(8,128)} async-done(((f32[1024,5,64]{0,2,1:T(8,128)}), f32[128,5,64]{0,2,1:T(8,128)}) %reduce-scatter.9.cloned.1.call-update) | async-done | bytes 163856 | tf_op jit(solution)/shard_map/reduce_scatter | solution.py:220
  749.0 25.8 %all-gather.50.cloned.1.call-done = bf16[1024,960]{0,1:T(8,128)(2,1)} async-done(((bf16[128,960]{0,1:T(8,128)(2,1)}), bf16[1024,960]{0,1:T(8,128)(2,1)}) %all-gather.50.cloned.1.call-update) | async-done | bytes 1966096 | tf_op jit(solution)/shard_map/all_gather | solution.py:241
  778.0 26.3 %all-gather.56.cloned.1.call-done = bf16[1024,960]{0,1:T(8,128)(2,1)} async-done(((bf16[128,960]{0,1:T(8,128)(2,1)}), bf16[1024,960]{0,1:T(8,128)(2,1)}) %all-gather.56.cloned.1.call-update) | async-done | bytes 1966096 | tf_op jit(solution)/shard_map/all_gather | solution.py:244
  804.3 30.1 %all-gather.58.cloned.1.call-done = bf16[1024,960]{0,1:T(8,128)(2,1)} async-done(((bf16[128,960]{0,1:T(8,128)(2,1)}), bf16[1024,960]{0,1:T(8,128)(2,1)}) %all-gather.58.cloned.1.call-update) | async-done | bytes 1966096 | tf_op jit(solution)/shard_map/all_gather | solution.py:245
  837.7 26.2 %all-gather.78.cloned.1.call-done = bf16[1024,960]{0,1:T(8,128)(2,1)} async-done(((bf16[128,960]{0,1:T(8,128)(2,1)}), bf16[1024,960]{0,1:T(8,128)(2,1)}) %all-gather.78.cloned.1.call-update) | async-done | bytes 1966096 | tf_op jit(solution)/shard_map/all_gather | solution.py:250
  864.0 42.9 %all-gather.76.cloned.1.call-done = bf16[1024,2560]{1,0:T(8,128)(2,1)} async-done(((bf16[128,2560]{1,0:T(8,128)(2,1)}), bf16[1024,2560]{1,0:T(8,128)(2,1)}) %all-gather.76.cloned.1.call-update) | async-done | bytes 5242896 | tf_op jit(solution)/shard_map/all_gather | solution.py:249
  911.2 25.2 %all-gather.102.cloned.1.call-done = bf16[1,1024,960]{1,2,0:T(8,128)(2,1)} async-done(((bf16[1,128,960]{1,2,0:T(8,128)(2,1)}), bf16[1,1024,960]{1,2,0:T(8,128)(2,1)}) %all-gather.102.cloned.1.call-update) | async-done | bytes 1966096 | tf_op jit(solution)/shard_map/all_gather | solution.py:250
  936.4 43.5 %all-gather.80.cloned.1.call-done = bf16[1024,2560]{1,0:T(8,128)(2,1)} async-done(((bf16[128,2560]{1,0:T(8,128)(2,1)}), bf16[1024,2560]{1,0:T(8,128)(2,1)}) %all-gather.80.cloned.1.call-update) | async-done | bytes 5242896 | tf_op jit(solution)/shard_map/all_gather | solution.py:249
  984.2 25.1 %all-gather.68.cloned.1.call-done = bf16[1024,960]{0,1:T(8,128)(2,1)} async-done(((bf16[128,960]{0,1:T(8,128)(2,1)}), bf16[1024,960]{0,1:T(8,128)(2,1)}) %all-gather.68.cloned.1.call-update) | async-done | bytes 1966096 | tf_op jit(solution)/shard_map/all_gather | solution.py:246
  1009.2 43.6 %all-gather.74.cloned.1.call-done = bf16[1024,2560]{1,0:T(8,128)(2,1)} async-done(((bf16[128,2560]{1,0:T(8,128)(2,1)}), bf16[1024,2560]{1,0:T(8,128)(2,1)}) %all-gather.74.cloned.1.call-update) | async-done | bytes 5242896 | tf_op jit(solution)/shard_map/all_gather | solution.py:248
  1057.3 39.1 %all-gather.70.cloned.1.call-done = bf16[1024,2560]{1,0:T(8,128)(2,1)} async-done(((bf16[128,2560]{1,0:T(8,128)(2,1)}), bf16[1024,2560]{1,0:T(8,128)(2,1)}) %all-gather.70.cloned.1.call-update) | async-done | bytes 5242896 | tf_op jit(solution)/shard_map/all_gather | solution.py:247
  1101.0 24.9 %all-gather.64.cloned.1.call-done = bf16[1024,960]{0,1:T(8,128)(2,1)} async-done(((bf16[128,960]{0,1:T(8,128)(2,1)}), bf16[1024,960]{0,1:T(8,128)(2,1)}) %all-gather.64.cloned.1.call-update) | async-done | bytes 1966096 | tf_op jit(solution)/shard_map/all_gather | solution.py:246
  1125.8 43.0 %all-gather.72.cloned.1.call-done = bf16[1024,2560]{1,0:T(8,128)(2,1)} async-done(((bf16[128,2560]{1,0:T(8,128)(2,1)}), bf16[1024,2560]{1,0:T(8,128)(2,1)}) %all-gather.72.cloned.1.call-update) | async-done | bytes 5242896 | tf_op jit(solution)/shard_map/all_gather | solution.py:248
  1173.5 38.4 %all-gather.66.cloned.1.call-done = bf16[1024,2560]{1,0:T(8,128)(2,1)} async-done(((bf16[128,2560]{1,0:T(8,128)(2,1)}), bf16[1024,2560]{1,0:T(8,128)(2,1)}) %all-gather.66.cloned.1.call-update) | async-done | bytes 5242896 | tf_op jit(solution)/shard_map/all_gather | solution.py:247
  1225.3 24.6 %all-reduce.8 = (f32[960]{0:T(1024)S(1)}, f32[960]{0:T(1024)S(1)}, f32[960]{0:T(1024)S(1)}, f32[960]{0:T(1024)S(1)}) all-reduce(f32[960]{0:T(1024)S(1)} %copy-done.74, f32[960]{0:T(1024)S(1)} %get-tuple-element.17, f32[960]{0:T(1024)S(1)} %copy-done.73, f32[960]{0:T(1024)S(1)} %copy-done.75), channel_id=26, replica_groups=mesh['group'=8,'replica'=4] {'group'}, use_global_device_ids=true, to_apply=%region_22.23.clone | all-reduce | flops 3840 | bytes 30720
  1264.0 311.0 %all-reduce.14.cloned.1.call-done = (f32[1,120,960]{2,1,0:T(8,128)}, f32[1,120,960]{2,1,0:T(8,128)}, f32[1,120,320]{1,2,0:T(8,128)}, f32[1,120,320]{1,2,0:T(8,12...) async-done(((f32[1,120,960]{2,1,0:T(8,128)}, ...) | async-done | bytes 9830416 | tf_op jit(solution)/shard_map/psum | solution.py:140
  (413 shorter events, 368.8 us)
Async XLA Ops:
  7.2 129.2 %all-gather.82.cloned.1.call-start = ((), (), s32[]{:S(2)}) async-start(), calls=%async_computation.25 | async-start | bytes 2211840 | tf_op jit(solution)/shard_map/all_gather | solution.py:305
  9.2 143.5 %all-gather.84.cloned.1.call-start = ((), (), s32[]{:S(2)}) async-start(), calls=%async_computation.26 | async-start | bytes 2211840 | tf_op jit(solution)/shard_map/all_gather | solution.py:308
  11.3 144.2 %all-gather.86.cloned.1.call-start = ((), (), s32[]{:S(2)}) async-start(), calls=%async_computation.27 | async-start | bytes 5529600 | tf_op jit(solution)/shard_map/all_gather | solution.py:310
  12.5 149.3 %all-gather.88.cloned.1.call-start = ((), (), s32[]{:S(2)}) async-start(), calls=%async_computation.28 | async-start | bytes 5529600 | tf_op jit(solution)/shard_map/all_gather | solution.py:311
  13.7 191.5 %all-gather.90.cloned.1.call-start = ((), (), s32[]{:S(2)}) async-start(), calls=%async_computation.29 | async-start | bytes 5898240 | tf_op jit(solution)/shard_map/all_gather | solution.py:312
  15.4 223.4 %all-gather.92.cloned.1.call-start = ((), (), s32[]{:S(2)}) async-start(), calls=%async_computation.30 | async-start | bytes 2211840 | tf_op jit(solution)/shard_map/all_gather | solution.py:305
  16.0 252.7 %all-gather.94.cloned.1.call-start = ((), (), s32[]{:S(2)}) async-start(), calls=%async_computation.31 | async-start | bytes 2211840 | tf_op jit(solution)/shard_map/all_gather | solution.py:308
  16.7 294.2 %all-gather.98.cloned.1.call-start = ((), (), s32[]{:S(2)}) async-start(), calls=%async_computation.33 | async-start | bytes 5529600 | tf_op jit(solution)/shard_map/all_gather | solution.py:311
  17.5 337.1 %all-gather.100.cloned.1.call-start = ((), (), s32[]{:S(2)}) async-start(), calls=%async_computation.34 | async-start | bytes 5898240 | tf_op jit(solution)/shard_map/all_gather | solution.py:312
  18.2 377.9 %all-gather.96.cloned.1.call-start = ((), (), s32[]{:S(2)}) async-start(), calls=%async_computation.32 | async-start | bytes 5529600 | tf_op jit(solution)/shard_map/all_gather | solution.py:310
  18.8 452.7 %reduce-scatter.5.cloned.1.call-start = ((), (), s32[]{:S(2)}) async-start(), calls=%async_computation.4 | async-start | bytes 1474560 | tf_op jit(solution)/shard_map/reduce_scatter | solution.py:220
  439.8 161.0 %all-gather.52.cloned.1.call-start = ((), (), s32[]{:S(2)}) async-start(), calls=%async_computation.10 | async-start | bytes 2211840 | tf_op jit(solution)/shard_map/all_gather | solution.py:240
  440.5 164.4 %all-gather.54.cloned.1.call-start = ((), (), s32[]{:S(2)}) async-start(), calls=%async_computation.11 | async-start | bytes 2211840 | tf_op jit(solution)/shard_map/all_gather | solution.py:241
  444.6 163.5 %all-gather.62.cloned.1.call-start = ((), (), s32[]{:S(2)}) async-start(), calls=%async_computation.15 | async-start | bytes 2211840 | tf_op jit(solution)/shard_map/all_gather | solution.py:245
  445.2 188.1 %all-gather.60.cloned.1.call-start = ((), (), s32[]{:S(2)}) async-start(), calls=%async_computation.14 | async-start | bytes 2211840 | tf_op jit(solution)/shard_map/all_gather | solution.py:244
  445.8 228.5 %reduce-scatter.11.cloned.1.call-start = ((), (), s32[]{:S(2)}) async-start(), calls=%async_computation.7 | async-start | bytes 1474560 | tf_op jit(solution)/shard_map/reduce_scatter | solution.py:221
  544.6 170.7 %reduce-scatter.9.cloned.1.call-start = ((), (), s32[]{:S(2)}) async-start(), calls=%async_computation.6 | async-start | bytes 1474560 | tf_op jit(solution)/shard_map/reduce_scatter | solution.py:220
  563.6 181.3 %all-gather.48.cloned.1.call-start = ((), (), s32[]{:S(2)}) async-start(), calls=%async_computation.8 | async-start | bytes 2211840 | tf_op jit(solution)/shard_map/all_gather | solution.py:240
  564.3 210.5 %all-gather.50.cloned.1.call-start = ((), (), s32[]{:S(2)}) async-start(), calls=%async_computation.9 | async-start | bytes 2211840 | tf_op jit(solution)/shard_map/all_gather | solution.py:241
  568.3 236.0 %all-gather.56.cloned.1.call-start = ((), (), s32[]{:S(2)}) async-start(), calls=%async_computation.12 | async-start | bytes 2211840 | tf_op jit(solution)/shard_map/all_gather | solution.py:244
  569.0 265.4 %all-gather.58.cloned.1.call-start = ((), (), s32[]{:S(2)}) async-start(), calls=%async_computation.13 | async-start | bytes 2211840 | tf_op jit(solution)/shard_map/all_gather | solution.py:245
  569.8 294.2 %all-gather.78.cloned.1.call-start = ((), (), s32[]{:S(2)}) async-start(), calls=%async_computation.23 | async-start | bytes 2211840 | tf_op jit(solution)/shard_map/all_gather | solution.py:250
  570.5 336.3 %all-gather.76.cloned.1.call-start = ((), (), s32[]{:S(2)}) async-start(), calls=%async_computation.22 | async-start | bytes 5898240 | tf_op jit(solution)/shard_map/all_gather | solution.py:249
  571.1 365.3 %all-gather.102.cloned.1.call-start = ((), (), s32[]{:S(2)}) async-start(), calls=%async_computation.35 | async-start | bytes 2211840 | tf_op jit(solution)/shard_map/all_gather | solution.py:250
  571.9 408.0 %all-gather.80.cloned.1.call-start = ((), (), s32[]{:S(2)}) async-start(), calls=%async_computation.24 | async-start | bytes 5898240 | tf_op jit(solution)/shard_map/all_gather | solution.py:249
  572.4 436.8 %all-gather.68.cloned.1.call-start = ((), (), s32[]{:S(2)}) async-start(), calls=%async_computation.18 | async-start | bytes 2211840 | tf_op jit(solution)/shard_map/all_gather | solution.py:246
  573.0 479.8 %all-gather.74.cloned.1.call-start = ((), (), s32[]{:S(2)}) async-start(), calls=%async_computation.21 | async-start | bytes 5898240 | tf_op jit(solution)/shard_map/all_gather | solution.py:248
  573.8 522.7 %all-gather.70.cloned.1.call-start = ((), (), s32[]{:S(2)}) async-start(), calls=%async_computation.19 | async-start | bytes 5898240 | tf_op jit(solution)/shard_map/all_gather | solution.py:247
  574.5 551.3 %all-gather.64.cloned.1.call-start = ((), (), s32[]{:S(2)}) async-start(), calls=%async_computation.16 | async-start | bytes 2211840 | tf_op jit(solution)/shard_map/all_gather | solution.py:246
  575.1 593.8 %all-gather.72.cloned.1.call-start = ((), (), s32[]{:S(2)}) async-start(), calls=%async_computation.20 | async-start | bytes 5898240 | tf_op jit(solution)/shard_map/all_gather | solution.py:248
  575.8 636.1 %all-gather.66.cloned.1.call-start = ((), (), s32[]{:S(2)}) async-start(), calls=%async_computation.17 | async-start | bytes 5898240 | tf_op jit(solution)/shard_map/all_gather | solution.py:247
  576.6 998.4 %all-reduce.14.cloned.1.call-start = ((), (), s32[]{:S(2)}) async-start(), calls=%async_computation.36 | async-start | bytes 20316160 | tf_op jit(solution)/shard_map/psum | solution.py:140
  (97 other events, 1151.4 us)
Sparse Core Ops, SparseCore 0:
  10.5 30.1 all-gather.81
  72.4 47.8 all-gather.85
  122.0 39.7 all-gather.87
  164.1 41.1 all-gather.89
  207.5 31.2 all-gather.91
  241.3 27.4 all-gather.93
  271.2 39.7 all-gather.97
  313.4 41.1 all-gather.99
  356.3 39.7 all-gather.95
  434.1 37.3 reduce-scatter.4
  475.2 37.3 reduce-scatter.6
  514.4 27.5 all-gather.51
  544.4 27.6 all-gather.53
  573.7 30.1 all-gather.61
  605.7 27.5 all-gather.59
  636.9 37.3 reduce-scatter.10
  678.0 37.3 reduce-scatter.8
  717.2 27.5 all-gather.47
  747.1 27.6 all-gather.49
  776.7 27.6 all-gather.55
  806.8 27.6 all-gather.57
  836.3 27.6 all-gather.77
  865.7 41.1 all-gather.75
  908.7 27.6 all-gather.101
  938.7 41.1 all-gather.79
  981.6 27.6 all-gather.67
  1011.7 41.1 all-gather.73
  1055.3 41.1 all-gather.69
  1098.2 27.6 all-gather.63
  1127.7 41.1 all-gather.71
  1170.7 41.1 all-gather.65
  1217.5 357.5 all-reduce.13
  (1 shorter events, 27.3 us)
where the time goes:
time: 1600 us; the launch traced here: 1590 us
  waiting for transfers between devices  1100 us (69%)
  blocking collectives  205 us (13%)
  matrix products  191 us (12%)
  other arithmetic  38.1 us (2%)
  local copies, waits for them, and re-layouts  36.4 us (2%)
  between operations  17.4 us (1%)
    psum x1, waiting for transfers between devices, replica_total(): lax.psum((share_gain_attn, share_query, share_key, share_value, share_out...  311 us
    all_gather x2, waiting for transfers between devices, layer_backward(): piece_up = lax.all_gather(grad_up_low, 'group', axis=0, tiled=True)  86.6 us
    all_gather x2, waiting for transfers between devices, layer_backward(): piece_hidden = lax.all_gather(hidden, 'group', axis=0, tiled=True)  86.4 us
    all_gather x2, waiting for transfers between devices, on_device(): lax.all_gather(w_down[layer_index], 'group', axis=0, tiled=True)  78 us
    all_gather x2, waiting for transfers between devices, layer_backward(): piece_gate = lax.all_gather(grad_gate_low, 'group', axis=0, tiled=True)  77.5 us
    reduce_scatter x2, waiting for transfers between devices, layer_backward(): lax.psum_scatter(grad_value_all, 'group', scatter_dimension=0, tiled=True)  75.5 us
    reduce_scatter x2, waiting for transfers between devices, layer_backward(): lax.psum_scatter(grad_key_all, 'group', scatter_dimension=0, tiled=True)  65.6 us
    all_gather x2, waiting for transfers between devices, layer_backward(): piece_branch = lax.all_gather(branch_low, 'group', axis=0, tiled=True)  51.5 us
  transfers between devices with their start and end apart: 33, of which 27 were waited for; matrix products, arithmetic and copies ran while one was open for 13% of the time, Pallas kernels for 0%

commit v1 on v0

--- a/solution.py
+++ b/solution.py
@@ -243,7 +243,13 @@
     piece_value = lax.all_gather(value_back, "group", axis=0, tiled=True)
     piece_mixed = lax.all_gather(mixed_heads, "group", axis=0, tiled=True)
     piece_after = lax.all_gather(after_low, "group", axis=0, tiled=True)
-    piece_ffn = lax.all_gather(normed_ffn, "group", axis=0, tiled=True)
+    peers = lax.axis_size("group")
+    current, blocks = (normed_ffn, [normed_ffn])
+    for _ in range(peers - 1):
+        current = lax.ppermute(current, "group", [(i, (i + 1) % peers) for i in range(peers)])
+        blocks.insert(0, current)
+    line = jnp.concatenate(blocks, axis=0)
+    piece_ffn = jnp.roll(line, (lax.axis_index("group") + 1) * normed_ffn.shape[0], axis=0)
     piece_gate = lax.all_gather(grad_gate_low, "group", axis=0, tiled=True)
     piece_up = lax.all_gather(grad_up_low, "group", axis=0, tiled=True)
     piece_hidden = lax.all_gather(hidden, "group", axis=0, tiled=True)

time: 1600 us -> 1540 us (0.963)
  waiting for transfers between devices: 1100 us -> 1020 us
    ppermute x0 -> x14, waiting for transfers between devices: none -> 68.9 us  [layer_backward(): lax.ppermute(current, 'group', [(i, (i + 1) % peers) for i in range(peers)])]
    reduce_scatter x2, waiting for transfers between devices: 75.5 us -> 12 us  [layer_backward(): lax.psum_scatter(grad_value_all, 'group', scatter_dimension=0, tiled=True)]
    all_gather x2 -> x0, waiting for transfers between devices: 49.9 us -> none  [layer_backward(): piece_ffn = lax.all_gather(normed_ffn, 'group', axis=0, tiled=True)]
    all_gather x2, waiting for transfers between devices: 51.4 us -> 26.3 us  [layer_backward(): piece_mixed = lax.all_gather(mixed_heads, 'group', axis=0, tiled=True)]
  transfers between devices with their start and end apart: 33 -> 45, of which waited for: 27 -> 36; matrix products, arithmetic and copies ran while one was open for 13% -> 15% of each run, Pallas kernels for 0% -> 0%
where the time goes in v1:
time: 1540 us; the launch traced here: 1530 us
  waiting for transfers between devices  1020 us (66%)
  blocking collectives  208 us (14%)
  matrix products  190 us (12%)
  local copies, waits for them, and re-layouts  48.1 us (3%)
  other arithmetic  38.8 us (3%)
  between operations  17.7 us (1%)
    psum x1, waiting for transfers between devices, replica_total(): lax.psum((share_gain_attn, share_query, share_key, share_value, share_out...  311 us
    all_gather x2, waiting for transfers between devices, layer_backward(): piece_hidden = lax.all_gather(hidden, 'group', axis=0, tiled=True)  86.4 us
    all_gather x2, waiting for transfers between devices, layer_backward(): piece_gate = lax.all_gather(grad_gate_low, 'group', axis=0, tiled=True)  78.1 us
    all_gather x2, waiting for transfers between devices, layer_backward(): piece_up = lax.all_gather(grad_up_low, 'group', axis=0, tiled=True)  76.7 us
    all_gather x2, waiting for transfers between devices, on_device(): lax.all_gather(w_down[layer_index], 'group', axis=0, tiled=True)  73 us
    reduce_scatter x2, waiting for transfers between devices, layer_backward(): lax.psum_scatter(grad_key_all, 'group', scatter_dimension=0, tiled=True)  71.2 us
    ppermute x14, waiting for transfers between devices, layer_backward(): lax.ppermute(current, 'group', [(i, (i + 1) % peers) for i in range(peers)])  68.9 us
    all_gather x2, waiting for transfers between devices, layer_backward(): piece_branch = lax.all_gather(branch_low, 'group', axis=0, tiled=True)  51.5 us
  transfers between devices with their start and end apart: 45, of which 36 were waited for; matrix products, arithmetic and copies ran while one was open for 15% of the time, Pallas kernels for 0%

profile of v1, /device:TPU:0, one launch (start us, length us, event | category | flops | bytes accessed | tf_op | source)
XLA Modules:
  0.0 1527.6 jit_solution(2595228946666722594)
XLA Ops:
  21.0 15.6 %all-reduce.11 = (bf16[960]{0:T(1024)(128)(2,1)S(1)}, bf16[960]{0:T(1024)(128)(2,1)S(1)}, bf16[960]{0:T(1024)(128)(2,1)S(1)}, bf16[960]{0:T(1024)(128)(2,1)S(1)}) all-reduce(bf16[960]{0:T(1024)(128)(2,1)S(1)} %dynamic-update-slice, bf16[960]{0:T(1024)(128)(2,1)S(1)} %dynamic-update-slice.1, ...), channel_id=2, replica_groups=mesh['group'=8,'replica'=4] {'group'}, use_global_device_ids=true, to_apply=%add | all-reduce | flops 3840 | bytes 15360
  37.1 12.7 all-gather.1
  64.9 15.5 %all-gather.2 = bf16[1,960,320]{2,0,1:T(2,128)(2,1)} all-gather(bf16[1,120,320]{2,0,1:T(2,128)(2,1)S(1)} %copy.80), channel_id=4, replica_groups=mesh['group'=8,'replica'=4] {'group'}, dimensions={1}, use_global_device_ids=true | all-gather | bytes 691200 | tf_op jit(solution)/shard_map/all_gather | solution.py:312
  84.6 11.0 all_gather.152
  96.5 20.6 %all-gather.10 = bf16[1,960,320]{2,0,1:T(2,128)(2,1)} all-gather(bf16[1,120,320]{2,0,1:T(2,128)(2,1)S(1)} %copy.81), channel_id=12, replica_groups=mesh['group'=8,'replica'=4] {'group'}, dimensions={1}, use_global_device_ids=true | all-gather | bytes 691200 | tf_op jit(solution)/shard_map/all_gather | solution.py:313
  121.9 18.1 %all-gather.11 = bf16[1,960,320]{2,0,1:T(2,128)(2,1)} all-gather(bf16[1,120,320]{2,0,1:T(2,128)(2,1)S(1)} %copy.82), channel_id=13, replica_groups=mesh['group'=8,'replica'=4] {'group'}, dimensions={1}, use_global_device_ids=true | all-gather | bytes 691200 | tf_op jit(solution)/shard_map/all_gather | solution.py:312
  173.6 33.8 %all-gather.84.cloned.1.call-done = bf16[1,2560,960]{2,1,0:T(8,128)(2,1)} async-done(((bf16[1,320,960]{2,1,0:T(8,128)(2,1)}), bf16[1,2560,960]{2,1,0:T(8,128)(2,1)}) %all-gather.84.cloned.1.call-update) | async-done | bytes 4915216 | tf_op jit(solution)/shard_map/all_gather | solution.py:318
  213.9 11.9 all_gather.161
  225.8 13.8 all_gather.163
  254.0 16.2 %all-gather.88.cloned.1.call-done = bf16[1,960,960]{2,1,0:T(8,128)(2,1)} async-done(((bf16[1,120,960]{2,1,0:T(8,128)(2,1)}), bf16[1,960,960]{2,1,0:T(8,128)(2,1)}) %all-gather.88.cloned.1.call-update) | async-done | bytes 1843216 | tf_op jit(solution)/shard_map/all_gather | solution.py:314
  272.9 39.5 %all-gather.92.cloned.1.call-done = bf16[1,960,2560]{2,1,0:T(8,128)(2,1)} async-done(((bf16[1,120,2560]{2,1,0:T(8,128)(2,1)}), bf16[1,960,2560]{2,1,0:T(8,128)(2,1)}) %all-gather.92.cloned.1.call-update) | async-done | bytes 4915216 | tf_op jit(solution)/shard_map/all_gather | solution.py:317
  316.8 39.2 %all-gather.94.cloned.1.call-done = bf16[1,2560,960]{2,1,0:T(8,128)(2,1)} async-done(((bf16[1,320,960]{2,1,0:T(8,128)(2,1)}), bf16[1,2560,960]{2,1,0:T(8,128)(2,1)}) %all-gather.94.cloned.1.call-update) | async-done | bytes 4915216 | tf_op jit(solution)/shard_map/all_gather | solution.py:318
  361.5 36.1 %all-gather.90.cloned.1.call-done = bf16[1,960,2560]{2,1,0:T(8,128)(2,1)} async-done(((bf16[1,120,2560]{2,1,0:T(8,128)(2,1)}), bf16[1,960,2560]{2,1,0:T(8,128)(2,1)}) %all-gather.90.cloned.1.call-update) | async-done | bytes 4915216 | tf_op jit(solution)/shard_map/all_gather | solution.py:316
  448.2 12.0 reduce-scatter.7.cloned.1.call-done
  464.1 36.6 %reduce-scatter.5.cloned.1.call-done = f32[128,5,64]{0,2,1:T(8,128)} async-done(((f32[1024,5,64]{0,2,1:T(8,128)}), f32[128,5,64]{0,2,1:T(8,128)}) %reduce-scatter.5.cloned.1.call-update) | async-done | bytes 163856 | tf_op jit(solution)/shard_map/reduce_scatter | solution.py:220
  650.7 12.0 all_gather.177
  674.3 34.6 %reduce-scatter.9.cloned.1.call-done = f32[128,5,64]{0,2,1:T(8,128)} async-done(((f32[1024,5,64]{0,2,1:T(8,128)}), f32[128,5,64]{0,2,1:T(8,128)}) %reduce-scatter.9.cloned.1.call-update) | async-done | bytes 163856 | tf_op jit(solution)/shard_map/reduce_scatter | solution.py:220
  709.9 11.2 all_gather.174
  742.7 25.2 %all-gather.48.cloned.1.call-done = bf16[1024,960]{0,1:T(8,128)(2,1)} async-done(((bf16[128,960]{0,1:T(8,128)(2,1)}), bf16[1024,960]{0,1:T(8,128)(2,1)}) %all-gather.48.cloned.1.call-update) | async-done | bytes 1966096 | tf_op jit(solution)/shard_map/all_gather | solution.py:241
  771.1 26.3 %all-gather.54.cloned.1.call-done = bf16[1024,960]{0,1:T(8,128)(2,1)} async-done(((bf16[128,960]{0,1:T(8,128)(2,1)}), bf16[1024,960]{0,1:T(8,128)(2,1)}) %all-gather.54.cloned.1.call-update) | async-done | bytes 1966096 | tf_op jit(solution)/shard_map/all_gather | solution.py:244
  797.4 29.5 %all-gather.56.cloned.1.call-done = bf16[1024,960]{0,1:T(8,128)(2,1)} async-done(((bf16[128,960]{0,1:T(8,128)(2,1)}), bf16[1024,960]{0,1:T(8,128)(2,1)}) %all-gather.56.cloned.1.call-update) | async-done | bytes 1966096 | tf_op jit(solution)/shard_map/all_gather | solution.py:245
  830.2 26.3 %all-gather.96.cloned.1.call-done = bf16[1,1024,960]{1,2,0:T(8,128)(2,1)} async-done(((bf16[1,128,960]{1,2,0:T(8,128)(2,1)}), bf16[1,1024,960]{1,2,0:T(8,128)(2,1)}) %all-gather.96.cloned.1.call-update) | async-done | bytes 1966096 | tf_op jit(solution)/shard_map/all_gather | solution.py:256
  856.4 43.5 %all-gather.74.cloned.1.call-done = bf16[1024,2560]{1,0:T(8,128)(2,1)} async-done(((bf16[128,2560]{1,0:T(8,128)(2,1)}), bf16[1024,2560]{1,0:T(8,128)(2,1)}) %all-gather.74.cloned.1.call-update) | async-done | bytes 5242896 | tf_op jit(solution)/shard_map/all_gather | solution.py:255
  904.2 25.2 %all-gather.72.cloned.1.call-done = bf16[1024,960]{0,1:T(8,128)(2,1)} async-done(((bf16[128,960]{0,1:T(8,128)(2,1)}), bf16[1024,960]{0,1:T(8,128)(2,1)}) %all-gather.72.cloned.1.call-update) | async-done | bytes 1966096 | tf_op jit(solution)/shard_map/all_gather | solution.py:256
  929.4 42.9 %all-gather.70.cloned.1.call-done = bf16[1024,2560]{1,0:T(8,128)(2,1)} async-done(((bf16[128,2560]{1,0:T(8,128)(2,1)}), bf16[1024,2560]{1,0:T(8,128)(2,1)}) %all-gather.70.cloned.1.call-update) | async-done | bytes 5242896 | tf_op jit(solution)/shard_map/all_gather | solution.py:255
  976.6 39.1 %all-gather.64.cloned.1.call-done = bf16[1024,2560]{1,0:T(8,128)(2,1)} async-done(((bf16[128,2560]{1,0:T(8,128)(2,1)}), bf16[1024,2560]{1,0:T(8,128)(2,1)}) %all-gather.64.cloned.1.call-update) | async-done | bytes 5242896 | tf_op jit(solution)/shard_map/all_gather | solution.py:253
  1020.4 38.4 %all-gather.68.cloned.1.call-done = bf16[1024,2560]{1,0:T(8,128)(2,1)} async-done(((bf16[128,2560]{1,0:T(8,128)(2,1)}), bf16[1024,2560]{1,0:T(8,128)(2,1)}) %all-gather.68.cloned.1.call-update) | async-done | bytes 5242896 | tf_op jit(solution)/shard_map/all_gather | solution.py:254
  1063.4 39.0 %all-gather.62.cloned.1.call-done = bf16[1024,2560]{1,0:T(8,128)(2,1)} async-done(((bf16[128,2560]{1,0:T(8,128)(2,1)}), bf16[1024,2560]{1,0:T(8,128)(2,1)}) %all-gather.62.cloned.1.call-update) | async-done | bytes 5242896 | tf_op jit(solution)/shard_map/all_gather | solution.py:253
  1107.0 38.3 %all-gather.66.cloned.1.call-done = bf16[1024,2560]{1,0:T(8,128)(2,1)} async-done(((bf16[128,2560]{1,0:T(8,128)(2,1)}), bf16[1024,2560]{1,0:T(8,128)(2,1)}) %all-gather.66.cloned.1.call-update) | async-done | bytes 5242896 | tf_op jit(solution)/shard_map/all_gather | solution.py:254
  1158.7 24.6 %all-reduce.8 = (f32[960]{0:T(1024)S(1)}, f32[960]{0:T(1024)S(1)}, f32[960]{0:T(1024)S(1)}, f32[960]{0:T(1024)S(1)}) all-reduce(f32[960]{0:T(1024)S(1)} %copy-done.84, f32[960]{0:T(1024)S(1)} %get-tuple-element.18, f32[960]{0:T(1024)S(1)} %copy-done.83, f32[960]{0:T(1024)S(1)} %copy-done.85), channel_id=26, replica_groups=mesh['group'=8,'replica'=4] {'group'}, use_global_device_ids=true, to_apply=%region_22.23.clone | all-reduce | flops 3840 | bytes 30720
  1183.6 11.7 all-reduce.9
  1197.4 311.2 %all-reduce.14.cloned.1.call-done = (f32[1,120,960]{2,1,0:T(8,128)}, f32[1,120,960]{2,1,0:T(8,128)}, f32[1,120,320]{1,2,0:T(8,128)}, f32[1,120,320]{1,2,0:T(8,12...) async-done(((f32[1,120,960]{2,1,0:T(8,128)}, ...) | async-done | bytes 9830416 | tf_op jit(solution)/shard_map/psum | solution.py:140
  (475 shorter events, 398.3 us)
Async XLA Ops:
  7.2 138.2 %all-gather.76.cloned.1.call-start = ((), (), s32[]{:S(2)}) async-start(), calls=%async_computation.23 | async-start | bytes 2211840 | tf_op jit(solution)/shard_map/all_gather | solution.py:311
  9.2 152.4 %all-gather.78.cloned.1.call-start = ((), (), s32[]{:S(2)}) async-start(), calls=%async_computation.24 | async-start | bytes 2211840 | tf_op jit(solution)/shard_map/all_gather | solution.py:314
  11.3 153.2 %all-gather.80.cloned.1.call-start = ((), (), s32[]{:S(2)}) async-start(), calls=%async_computation.25 | async-start | bytes 5529600 | tf_op jit(solution)/shard_map/all_gather | solution.py:316
  12.5 156.3 %all-gather.82.cloned.1.call-start = ((), (), s32[]{:S(2)}) async-start(), calls=%async_computation.26 | async-start | bytes 5529600 | tf_op jit(solution)/shard_map/all_gather | solution.py:317
  13.7 193.6 %all-gather.84.cloned.1.call-start = ((), (), s32[]{:S(2)}) async-start(), calls=%async_computation.27 | async-start | bytes 5898240 | tf_op jit(solution)/shard_map/all_gather | solution.py:318
  15.4 224.9 %all-gather.86.cloned.1.call-start = ((), (), s32[]{:S(2)}) async-start(), calls=%async_computation.28 | async-start | bytes 2211840 | tf_op jit(solution)/shard_map/all_gather | solution.py:311
  16.0 254.3 %all-gather.88.cloned.1.call-start = ((), (), s32[]{:S(2)}) async-start(), calls=%async_computation.29 | async-start | bytes 2211840 | tf_op jit(solution)/shard_map/all_gather | solution.py:314
  16.7 295.7 %all-gather.92.cloned.1.call-start = ((), (), s32[]{:S(2)}) async-start(), calls=%async_computation.31 | async-start | bytes 5529600 | tf_op jit(solution)/shard_map/all_gather | solution.py:317
  17.5 338.6 %all-gather.94.cloned.1.call-start = ((), (), s32[]{:S(2)}) async-start(), calls=%async_computation.32 | async-start | bytes 5898240 | tf_op jit(solution)/shard_map/all_gather | solution.py:318
  18.2 379.4 %all-gather.90.cloned.1.call-start = ((), (), s32[]{:S(2)}) async-start(), calls=%async_computation.30 | async-start | bytes 5529600 | tf_op jit(solution)/shard_map/all_gather | solution.py:316
  18.8 441.4 %reduce-scatter.7.cloned.1.call-start = ((), (), s32[]{:S(2)}) async-start(), calls=%async_computation.5 | async-start | bytes 1474560 | tf_op jit(solution)/shard_map/reduce_scatter | solution.py:221
  422.7 77.9 %reduce-scatter.5.cloned.1.call-start = ((), (), s32[]{:S(2)}) async-start(), calls=%async_computation.4 | async-start | bytes 1474560 | tf_op jit(solution)/shard_map/reduce_scatter | solution.py:220
  442.2 220.4 %all-gather.50.cloned.1.call-start = ((), (), s32[]{:S(2)}) async-start(), calls=%async_computation.10 | async-start | bytes 2211840 | tf_op jit(solution)/shard_map/all_gather | solution.py:240
  443.0 223.9 %all-gather.52.cloned.1.call-start = ((), (), s32[]{:S(2)}) async-start(), calls=%async_computation.11 | async-start | bytes 2211840 | tf_op jit(solution)/shard_map/all_gather | solution.py:241
  447.0 223.2 %all-gather.60.cloned.1.call-start = ((), (), s32[]{:S(2)}) async-start(), calls=%async_computation.15 | async-start | bytes 2211840 | tf_op jit(solution)/shard_map/all_gather | solution.py:245
  447.6 222.6 %all-gather.58.cloned.1.call-start = ((), (), s32[]{:S(2)}) async-start(), calls=%async_computation.14 | async-start | bytes 2211840 | tf_op jit(solution)/shard_map/all_gather | solution.py:244
  448.2 225.2 %reduce-scatter.11.cloned.1.call-start = ((), (), s32[]{:S(2)}) async-start(), calls=%async_computation.7 | async-start | bytes 1474560 | tf_op jit(solution)/shard_map/reduce_scatter | solution.py:221
  533.5 175.5 %reduce-scatter.9.cloned.1.call-start = ((), (), s32[]{:S(2)}) async-start(), calls=%async_computation.6 | async-start | bytes 1474560 | tf_op jit(solution)/shard_map/reduce_scatter | solution.py:220
  552.6 185.8 %all-gather.46.cloned.1.call-start = ((), (), s32[]{:S(2)}) async-start(), calls=%async_computation.8 | async-start | bytes 2211840 | tf_op jit(solution)/shard_map/all_gather | solution.py:240
  553.4 214.5 %all-gather.48.cloned.1.call-start = ((), (), s32[]{:S(2)}) async-start(), calls=%async_computation.9 | async-start | bytes 2211840 | tf_op jit(solution)/shard_map/all_gather | solution.py:241
  557.4 240.0 %all-gather.54.cloned.1.call-start = ((), (), s32[]{:S(2)}) async-start(), calls=%async_computation.12 | async-start | bytes 2211840 | tf_op jit(solution)/shard_map/all_gather | solution.py:244
  558.1 268.8 %all-gather.56.cloned.1.call-start = ((), (), s32[]{:S(2)}) async-start(), calls=%async_computation.13 | async-start | bytes 2211840 | tf_op jit(solution)/shard_map/all_gather | solution.py:245
  558.9 297.6 %all-gather.96.cloned.1.call-start = ((), (), s32[]{:S(2)}) async-start(), calls=%async_computation.33 | async-start | bytes 2211840 | tf_op jit(solution)/shard_map/all_gather | solution.py:256
  559.6 340.3 %all-gather.74.cloned.1.call-start = ((), (), s32[]{:S(2)}) async-start(), calls=%async_computation.22 | async-start | bytes 5898240 | tf_op jit(solution)/shard_map/all_gather | solution.py:255
  560.2 369.3 %all-gather.72.cloned.1.call-start = ((), (), s32[]{:S(2)}) async-start(), calls=%async_computation.21 | async-start | bytes 2211840 | tf_op jit(solution)/shard_map/all_gather | solution.py:256
  560.9 411.4 %all-gather.70.cloned.1.call-start = ((), (), s32[]{:S(2)}) async-start(), calls=%async_computation.20 | async-start | bytes 5898240 | tf_op jit(solution)/shard_map/all_gather | solution.py:255
  561.5 454.3 %all-gather.64.cloned.1.call-start = ((), (), s32[]{:S(2)}) async-start(), calls=%async_computation.17 | async-start | bytes 5898240 | tf_op jit(solution)/shard_map/all_gather | solution.py:253
  562.1 496.7 %all-gather.68.cloned.1.call-start = ((), (), s32[]{:S(2)}) async-start(), calls=%async_computation.19 | async-start | bytes 5898240 | tf_op jit(solution)/shard_map/all_gather | solution.py:254
  562.8 539.6 %all-gather.62.cloned.1.call-start = ((), (), s32[]{:S(2)}) async-start(), calls=%async_computation.16 | async-start | bytes 5898240 | tf_op jit(solution)/shard_map/all_gather | solution.py:253
  563.6 581.7 %all-gather.66.cloned.1.call-start = ((), (), s32[]{:S(2)}) async-start(), calls=%async_computation.18 | async-start | bytes 5898240 | tf_op jit(solution)/shard_map/all_gather | solution.py:254
  564.2 944.4 %all-reduce.14.cloned.1.call-start = ((), (), s32[]{:S(2)}) async-start(), calls=%async_computation.34 | async-start | bytes 20316160 | tf_op jit(solution)/shard_map/psum | solution.py:140
  578.1 14.4 collective-permute-start.7
  (121 other events, 1504.1 us)
Sparse Core Ops, SparseCore 0:
  10.5 30.1 all-gather.75
  42.5 27.3 all-gather.77
  72.4 46.8 all-gather.79
  121.0 42.8 all-gather.81
  166.2 41.1 all-gather.83
  209.7 30.6 all-gather.85
  242.8 27.3 all-gather.87
  272.7 39.7 all-gather.91
  314.9 41.1 all-gather.93
  357.8 39.7 all-gather.89
  422.8 37.3 reduce-scatter.6
  463.3 37.3 reduce-scatter.4
  502.5 27.5 all-gather.49
  531.9 27.6 all-gather.51
  561.8 32.5 all-gather.59
  596.2 31.3 all-gather.57
  631.2 37.3 reduce-scatter.10
  671.6 37.2 reduce-scatter.8
  710.8 27.5 all-gather.45
  740.2 27.6 all-gather.47
  769.7 27.6 all-gather.53
  799.3 27.6 all-gather.55
  828.8 27.6 all-gather.95
  858.8 41.1 all-gather.73
  901.8 27.6 all-gather.71
  931.2 41.1 all-gather.69
  974.6 41.1 all-gather.63
  1017.7 41.1 all-gather.67
  1061.3 41.1 all-gather.61
  1104.2 41.1 all-gather.65
  1151.0 357.5 all-reduce.13
